TPU v7x, 32 devices: a whole 2x2x4 slice. The times are simulated.
32 devices in a mesh: groups: 2 (over x), ctx: 8 (over z, y), head: 2 (over core).
Axes of the slice: x: 2, y: 2, z: 4, core: 2. Of those that a mesh axis runs over, the one named last changes fastest.
Arguments:
- queries: bfloat16 [4096, 4, 8, 128], P(('groups', 'ctx'), 'head'), parts along dimension 0, may hold values from -40 to 40
- keys: bfloat16 [4096, 4, 128], P(('groups', 'ctx'), 'head'), parts along dimension 0, may hold values from -6 to 6
- values: bfloat16 [4096, 4, 128], P(('groups', 'ctx'), 'head'), parts along dimension 0, may hold values from -6 to 6
- segments: int32 [4096], P(('groups', 'ctx')), parts along dimension 0, may hold values from 0 to 3, never falling along the last dimension, each value on 1 to 1024 neighbouring positions
- score_weight: bfloat16 [4, 8, 128], P('head'), may hold values from -0.09375 to 0.09375
Outputs:
- attended: bfloat16 [4096, 4, 8, 128], P(('groups', 'ctx'), 'head'), parts along dimension 0
- score: float32 [4096], P(('groups', 'ctx')), parts along dimension 0
There are 2 independent parts, one for each index of `groups`. A program takes and returns all parts, laid end to end along the dimension named above; an argument that names none is the same for every part. Nothing has to cross between parts.
Inputs may be any that keep to these rules, and one draw needn't show every extreme that they name: `segments`: document ids never fall along the sequence; each document covers 1 to 1024 positions and one covers exactly 1024.
All inputs are finite; a program needn't handle non-finite values.
Results may differ from a plain program's by a relative error of at most 0.0032.
Values may be sent and summed in bfloat16 or wider, within the bound.
No kernel may reach another device: no remote copies, remote signals or barrier semaphores. Data moves between devices by JAX's collectives and lax.ppermute only.
A program may use at most 64 MiB of HBM per device.

v0:
```python
import math

import jax
import jax.numpy as jnp
from jax import lax
from jax.sharding import PartitionSpec as P


def attend(query_rows, query_pos, query_seg, keys, values, segments):
    row_count, kv_local, group_size, head_dim = query_rows.shape
    tile = min(64, row_count)
    tile_count = row_count // tile
    root_dim = math.sqrt(head_dim)
    start_state = (
        jnp.full((row_count, kv_local, group_size), -1e30, jnp.float32),
        jnp.zeros((row_count, kv_local, group_size), jnp.float32),
        jnp.zeros((row_count, kv_local, group_size, head_dim), jnp.float32),
    )
    key_piece = lax.all_gather(keys, "ctx", axis=0, tiled=True)
    value_piece = lax.all_gather(values, "ctx", axis=0, tiled=True)
    seg_piece = lax.all_gather(segments, "ctx", axis=0, tiled=True)
    piece_rows = key_piece.shape[0]
    block = math.gcd(piece_rows, 512)

    def key_step(block_index, state):
        key_start = block_index * block
        key_block = lax.dynamic_slice_in_dim(key_piece, key_start, block, 0)
        value_block = lax.dynamic_slice_in_dim(value_piece, key_start, block, 0)
        seg_block = lax.dynamic_slice_in_dim(seg_piece, key_start, block, 0)
        key_pos = key_start + jnp.arange(block, dtype=jnp.int32)

        def query_step(tile_index, inner):
            row_start = tile_index * tile
            tile_pos = lax.dynamic_slice_in_dim(query_pos, row_start, tile, 0)
            tile_seg = lax.dynamic_slice_in_dim(query_seg, row_start, tile, 0)
            needed = (
                (key_pos[0] <= tile_pos[-1])
                & (seg_block[-1] >= tile_seg[0])
                & (seg_block[0] <= tile_seg[-1])
            )

            def compute(current):
                run_max, run_total, run_acc = current
                old_max = lax.dynamic_slice_in_dim(run_max, row_start, tile, 0)
                old_total = lax.dynamic_slice_in_dim(run_total, row_start, tile, 0)
                old_acc = lax.dynamic_slice_in_dim(run_acc, row_start, tile, 0)
                tile_query = lax.dynamic_slice_in_dim(query_rows, row_start, tile, 0)
                scores = (
                    jnp.einsum(
                        "qkgd,nkd->qkgn", tile_query, key_block, preferred_element_type=jnp.float32
                    )
                    / root_dim
                )
                allowed = (
                    (key_pos[None, :] <= tile_pos[:, None])
                    & (seg_block[None, :] == tile_seg[:, None])
                )[:, None, None, :]
                scores = jnp.where(allowed, scores, -1e30)
                new_max = jnp.maximum(old_max, jnp.max(scores, axis=-1))
                weights = jnp.where(allowed, jnp.exp(scores - new_max[..., None]), 0.0)
                factor = jnp.exp(old_max - new_max)
                new_total = old_total * factor + jnp.sum(weights, axis=-1)
                new_acc = old_acc * factor[..., None] + jnp.einsum(
                    "qkgn,nkd->qkgd",
                    weights.astype(jnp.bfloat16),
                    value_block,
                    preferred_element_type=jnp.float32,
                )
                return (
                    lax.dynamic_update_slice_in_dim(run_max, new_max, row_start, 0),
                    lax.dynamic_update_slice_in_dim(run_total, new_total, row_start, 0),
                    lax.dynamic_update_slice_in_dim(run_acc, new_acc, row_start, 0),
                )

            return lax.cond(needed, compute, lambda current: current, inner)

        return lax.fori_loop(0, tile_count, query_step, state)

    run_max, run_total, run_acc = lax.fori_loop(0, piece_rows // block, key_step, start_state)
    return (run_acc / run_total[..., None]).astype(jnp.bfloat16)


def local(queries, keys, values, segments, score_weight):
    row_count = queries.shape[0]
    my_index = lax.axis_index("ctx")
    local_rows = jnp.arange(row_count, dtype=jnp.int32)
    query_pos = my_index * row_count + local_rows
    attended = attend(queries, query_pos, segments, keys, values, segments)
    partial_score = jnp.einsum(
        "rkgd,kgd->r", attended, score_weight, preferred_element_type=jnp.float32
    )
    score = lax.psum(partial_score, "head")
    return (attended, score)


def solution(mesh):
    return jax.shard_map(
        local,
        mesh=mesh,
        in_specs=(
            P(("groups", "ctx"), "head", None, None),
            P(("groups", "ctx"), "head", None),
            P(("groups", "ctx"), "head", None),
            P(("groups", "ctx")),
            P("head", None, None),
        ),
        out_specs=(P(("groups", "ctx"), "head", None, None), P(("groups", "ctx"))),
        check_vma=False,
    )
```

profile of v0, /device:TPU:27, one launch (start us, length us, event | category | flops | bytes accessed | tf_op | source)
XLA Modules:
  0.0 252.0 jit_solution(440282068005692467)
XLA Ops:
  11.9 12.9 %all-gather = s32[8,1,256]{2,1,0:T(1,128)S(1)} all-gather(s32[1,1,256]{2,1,0:T(1,128)S(1)} %bitcast.41), channel_id=1, replica_groups=mesh['groups'=2,'ctx'=8,'head'=2] {'ctx'}, dimensions={0}, use_global_device_ids=true | all-gather | bytes 9216 | tf_op jit(solution)/shard_map/all_gather | solution.py:21
  24.8 23.9 %all-gather.4.cloned.1.call-done = bf16[2048,2,128]{2,0,1:T(8,128)(2,1)} async-done(((bf16[256,2,128]{2,0,1:T(8,128)(2,1)}), bf16[2048,2,128]{2,0,1:T(8,128)(2,1)}) %all-gather.4.cloned.1.call-update) | async-done | bytes 1048592 | tf_op jit(solution)/shard_map/all_gather | solution.py:19
  48.7 41.2 %all-gather.6.cloned.1.call-done = bf16[2048,2,128]{2,0,1:T(8,128)(2,1)} async-done(((bf16[256,2,128]{2,0,1:T(8,128)(2,1)}), bf16[2048,2,128]{2,0,1:T(8,128)(2,1)}) %all-gather.6.cloned.1.call-update) | async-done | bytes 1048592 | tf_op jit(solution)/shard_map/all_gather | solution.py:20
  91.4 145.9 %while.51 = (s32[]{:T(128)}, f32[256,2,8]{2,0,1:T(8,128)S(1)}, f32[256,2,8]{2,0,1:T(8,128)S(1)}, f32[256,2,8,128]{3,2,0,1:T(8,128)}, s32[2048]{0:T(1024)S(1)}, /...) while((s32[]{:T(128)}, f32[256,2,8]{2,0,1:T(8,128)S(1)}, ...), condition=%wide.region_7.8_spmd.clone, body=%wide.region_0.7_spmd.clone.sunk | while | flops 275614464 | bytes 10216774 | solution.py:79
  92.5 23.9 %while.52 = (s32[]{:T(128)}, f32[256,2,8]{2,0,1:T(8,128)S(1)}, f32[256,2,8]{2,0,1:T(8,128)S(1)}, f32[256,2,8,128]{3,2,0,1:T(8,128)}, s32[512]{0:T(512)S(1)}, /*i...) while((s32[]{:T(128)}, f32[256,2,8]{2,0,1:T(8,128)S(1)}, ...), condition=%wide.region_6.6_spmd, body=%wide.region_1.5_spmd.sunk | while | flops 275613696 | bytes 9160667 | solution.py:77
  117.6 37.6 %while.52 = (s32[]{:T(128)}, f32[256,2,8]{2,0,1:T(8,128)S(1)}, f32[256,2,8]{2,0,1:T(8,128)S(1)}, f32[256,2,8,128]{3,2,0,1:T(8,128)}, s32[512]{0:T(512)S(1)}, /*i...) while((s32[]{:T(128)}, f32[256,2,8]{2,0,1:T(8,128)S(1)}, ...), condition=%wide.region_6.6_spmd, body=%wide.region_1.5_spmd.sunk | while | flops 275613696 | bytes 9160667 | solution.py:77
  123.5 4.6 %conditional.2 = ((f32[256,2,8]{2,0,1:T(8,128)S(1)}, f32[256,2,8]{2,0,1:T(8,128)S(1)}, f32[256,2,8,128]{3,2,0,1:T(8,128)})) conditional(s32[]{:T(128)} %bitcast.38, (f32[256,2,8]{2,0,1:T(8,128)S(1)}, f32[256,2,8]{2,0,1:T(8,128)S(1)}, f32[256,2,8,128]{3,2,0,1:T(8,128)}) %tuple.87, (s32[]{:T(128)}, f32[256,2,8]{2,0,1:T(8,128)S(1)}, s32[512]{0:T(512)S(1)}, ...), branch_computations={%region_2.0_spmd, %region_3.4_spmd} | conditional | flops 275613696 | bytes 9159250 | solution.py:75
  134.1 4.6 %conditional.2 = ((f32[256,2,8]{2,0,1:T(8,128)S(1)}, f32[256,2,8]{2,0,1:T(8,128)S(1)}, f32[256,2,8,128]{3,2,0,1:T(8,128)})) conditional(s32[]{:T(128)} %bitcast.38, (f32[256,2,8]{2,0,1:T(8,128)S(1)}, f32[256,2,8]{2,0,1:T(8,128)S(1)}, f32[256,2,8,128]{3,2,0,1:T(8,128)}) %tuple.87, (s32[]{:T(128)}, f32[256,2,8]{2,0,1:T(8,128)S(1)}, s32[512]{0:T(512)S(1)}, ...), branch_computations={%region_2.0_spmd, %region_3.4_spmd} | conditional | flops 275613696 | bytes 9159250 | solution.py:75
  135.8 2.8 %fusion.7 = f32[256,2,8,128]{3,2,0,1:T(8,128)} fusion(f32[256,2,8,128]{3,2,0,1:T(8,128)} %get-tuple-element.403, s32[]{:T(128)S(6)} %select_n.30, f32[2,64,8,512]{3,2,1,0:T(8,128)S(1)} %get-tuple-element.533, f32[64,2,8]{2,0,1:T(8,128)S(1)} %get-tuple-element.531, pred[64,512]{1,0:T(8,128)(4,1)S(1)} %compare_and_fusion, ...), kind=kOutput, calls=%fused_computation.10 | convolution fusion | flops 137101312 | bytes 3604484 | tf_op jit(solution)/shard_map/while/body/eval_jaxpr/while/body/eval_jaxpr/cond/branch_1_fun/qkgn,nkd->qkgd/dot_general | solution.py:63
  144.6 4.6 %conditional.2 = ((f32[256,2,8]{2,0,1:T(8,128)S(1)}, f32[256,2,8]{2,0,1:T(8,128)S(1)}, f32[256,2,8,128]{3,2,0,1:T(8,128)})) conditional(s32[]{:T(128)} %bitcast.38, (f32[256,2,8]{2,0,1:T(8,128)S(1)}, f32[256,2,8]{2,0,1:T(8,128)S(1)}, f32[256,2,8,128]{3,2,0,1:T(8,128)}) %tuple.87, (s32[]{:T(128)}, f32[256,2,8]{2,0,1:T(8,128)S(1)}, s32[512]{0:T(512)S(1)}, ...), branch_computations={%region_2.0_spmd, %region_3.4_spmd} | conditional | flops 275613696 | bytes 9159250 | solution.py:75
  156.4 37.6 %while.52 = (s32[]{:T(128)}, f32[256,2,8]{2,0,1:T(8,128)S(1)}, f32[256,2,8]{2,0,1:T(8,128)S(1)}, f32[256,2,8,128]{3,2,0,1:T(8,128)}, s32[512]{0:T(512)S(1)}, /*i...) while((s32[]{:T(128)}, f32[256,2,8]{2,0,1:T(8,128)S(1)}, ...), condition=%wide.region_6.6_spmd, body=%wide.region_1.5_spmd.sunk | while | flops 275613696 | bytes 9160667 | solution.py:77
  162.3 4.6 %conditional.2 = ((f32[256,2,8]{2,0,1:T(8,128)S(1)}, f32[256,2,8]{2,0,1:T(8,128)S(1)}, f32[256,2,8,128]{3,2,0,1:T(8,128)})) conditional(s32[]{:T(128)} %bitcast.38, (f32[256,2,8]{2,0,1:T(8,128)S(1)}, f32[256,2,8]{2,0,1:T(8,128)S(1)}, f32[256,2,8,128]{3,2,0,1:T(8,128)}) %tuple.87, (s32[]{:T(128)}, f32[256,2,8]{2,0,1:T(8,128)S(1)}, s32[512]{0:T(512)S(1)}, ...), branch_computations={%region_2.0_spmd, %region_3.4_spmd} | conditional | flops 275613696 | bytes 9159250 | solution.py:75
  172.8 4.6 %conditional.2 = ((f32[256,2,8]{2,0,1:T(8,128)S(1)}, f32[256,2,8]{2,0,1:T(8,128)S(1)}, f32[256,2,8,128]{3,2,0,1:T(8,128)})) conditional(s32[]{:T(128)} %bitcast.38, (f32[256,2,8]{2,0,1:T(8,128)S(1)}, f32[256,2,8]{2,0,1:T(8,128)S(1)}, f32[256,2,8,128]{3,2,0,1:T(8,128)}) %tuple.87, (s32[]{:T(128)}, f32[256,2,8]{2,0,1:T(8,128)S(1)}, s32[512]{0:T(512)S(1)}, ...), branch_computations={%region_2.0_spmd, %region_3.4_spmd} | conditional | flops 275613696 | bytes 9159250 | solution.py:75
  174.6 2.8 %fusion.7 = f32[256,2,8,128]{3,2,0,1:T(8,128)} fusion(f32[256,2,8,128]{3,2,0,1:T(8,128)} %get-tuple-element.403, s32[]{:T(128)S(6)} %select_n.30, f32[2,64,8,512]{3,2,1,0:T(8,128)S(1)} %get-tuple-element.533, f32[64,2,8]{2,0,1:T(8,128)S(1)} %get-tuple-element.531, pred[64,512]{1,0:T(8,128)(4,1)S(1)} %compare_and_fusion, ...), kind=kOutput, calls=%fused_computation.10 | convolution fusion | flops 137101312 | bytes 3604484 | tf_op jit(solution)/shard_map/while/body/eval_jaxpr/while/body/eval_jaxpr/cond/branch_1_fun/qkgn,nkd->qkgd/dot_general | solution.py:63
  183.4 4.6 %conditional.2 = ((f32[256,2,8]{2,0,1:T(8,128)S(1)}, f32[256,2,8]{2,0,1:T(8,128)S(1)}, f32[256,2,8,128]{3,2,0,1:T(8,128)})) conditional(s32[]{:T(128)} %bitcast.38, (f32[256,2,8]{2,0,1:T(8,128)S(1)}, f32[256,2,8]{2,0,1:T(8,128)S(1)}, f32[256,2,8,128]{3,2,0,1:T(8,128)}) %tuple.87, (s32[]{:T(128)}, f32[256,2,8]{2,0,1:T(8,128)S(1)}, s32[512]{0:T(512)S(1)}, ...), branch_computations={%region_2.0_spmd, %region_3.4_spmd} | conditional | flops 275613696 | bytes 9159250 | solution.py:75
  195.1 42.2 %while.52 = (s32[]{:T(128)}, f32[256,2,8]{2,0,1:T(8,128)S(1)}, f32[256,2,8]{2,0,1:T(8,128)S(1)}, f32[256,2,8,128]{3,2,0,1:T(8,128)}, s32[512]{0:T(512)S(1)}, /*i...) while((s32[]{:T(128)}, f32[256,2,8]{2,0,1:T(8,128)S(1)}, ...), condition=%wide.region_6.6_spmd, body=%wide.region_1.5_spmd.sunk | while | flops 275613696 | bytes 9160667 | solution.py:77
  201.1 4.6 %conditional.2 = ((f32[256,2,8]{2,0,1:T(8,128)S(1)}, f32[256,2,8]{2,0,1:T(8,128)S(1)}, f32[256,2,8,128]{3,2,0,1:T(8,128)})) conditional(s32[]{:T(128)} %bitcast.38, (f32[256,2,8]{2,0,1:T(8,128)S(1)}, f32[256,2,8]{2,0,1:T(8,128)S(1)}, f32[256,2,8,128]{3,2,0,1:T(8,128)}) %tuple.87, (s32[]{:T(128)}, f32[256,2,8]{2,0,1:T(8,128)S(1)}, s32[512]{0:T(512)S(1)}, ...), branch_computations={%region_2.0_spmd, %region_3.4_spmd} | conditional | flops 275613696 | bytes 9159250 | solution.py:75
  202.8 2.8 %fusion.7 = f32[256,2,8,128]{3,2,0,1:T(8,128)} fusion(f32[256,2,8,128]{3,2,0,1:T(8,128)} %get-tuple-element.403, s32[]{:T(128)S(6)} %select_n.30, f32[2,64,8,512]{3,2,1,0:T(8,128)S(1)} %get-tuple-element.533, f32[64,2,8]{2,0,1:T(8,128)S(1)} %get-tuple-element.531, pred[64,512]{1,0:T(8,128)(4,1)S(1)} %compare_and_fusion, ...), kind=kOutput, calls=%fused_computation.10 | convolution fusion | flops 137101312 | bytes 3604484 | tf_op jit(solution)/shard_map/while/body/eval_jaxpr/while/body/eval_jaxpr/cond/branch_1_fun/qkgn,nkd->qkgd/dot_general | solution.py:63
  211.6 4.6 %conditional.2 = ((f32[256,2,8]{2,0,1:T(8,128)S(1)}, f32[256,2,8]{2,0,1:T(8,128)S(1)}, f32[256,2,8,128]{3,2,0,1:T(8,128)})) conditional(s32[]{:T(128)} %bitcast.38, (f32[256,2,8]{2,0,1:T(8,128)S(1)}, f32[256,2,8]{2,0,1:T(8,128)S(1)}, f32[256,2,8,128]{3,2,0,1:T(8,128)}) %tuple.87, (s32[]{:T(128)}, f32[256,2,8]{2,0,1:T(8,128)S(1)}, s32[512]{0:T(512)S(1)}, ...), branch_computations={%region_2.0_spmd, %region_3.4_spmd} | conditional | flops 275613696 | bytes 9159250 | solution.py:75
  213.4 2.8 %fusion.7 = f32[256,2,8,128]{3,2,0,1:T(8,128)} fusion(f32[256,2,8,128]{3,2,0,1:T(8,128)} %get-tuple-element.403, s32[]{:T(128)S(6)} %select_n.30, f32[2,64,8,512]{3,2,1,0:T(8,128)S(1)} %get-tuple-element.533, f32[64,2,8]{2,0,1:T(8,128)S(1)} %get-tuple-element.531, pred[64,512]{1,0:T(8,128)(4,1)S(1)} %compare_and_fusion, ...), kind=kOutput, calls=%fused_computation.10 | convolution fusion | flops 137101312 | bytes 3604484 | tf_op jit(solution)/shard_map/while/body/eval_jaxpr/while/body/eval_jaxpr/cond/branch_1_fun/qkgn,nkd->qkgd/dot_general | solution.py:63
  222.1 4.6 %conditional.2 = ((f32[256,2,8]{2,0,1:T(8,128)S(1)}, f32[256,2,8]{2,0,1:T(8,128)S(1)}, f32[256,2,8,128]{3,2,0,1:T(8,128)})) conditional(s32[]{:T(128)} %bitcast.38, (f32[256,2,8]{2,0,1:T(8,128)S(1)}, f32[256,2,8]{2,0,1:T(8,128)S(1)}, f32[256,2,8,128]{3,2,0,1:T(8,128)}) %tuple.87, (s32[]{:T(128)}, f32[256,2,8]{2,0,1:T(8,128)S(1)}, s32[512]{0:T(512)S(1)}, ...), branch_computations={%region_2.0_spmd, %region_3.4_spmd} | conditional | flops 275613696 | bytes 9159250 | solution.py:75
  232.7 4.6 %conditional.2 = ((f32[256,2,8]{2,0,1:T(8,128)S(1)}, f32[256,2,8]{2,0,1:T(8,128)S(1)}, f32[256,2,8,128]{3,2,0,1:T(8,128)})) conditional(s32[]{:T(128)} %bitcast.38, (f32[256,2,8]{2,0,1:T(8,128)S(1)}, f32[256,2,8]{2,0,1:T(8,128)S(1)}, f32[256,2,8,128]{3,2,0,1:T(8,128)}) %tuple.87, (s32[]{:T(128)}, f32[256,2,8]{2,0,1:T(8,128)S(1)}, s32[512]{0:T(512)S(1)}, ...), branch_computations={%region_2.0_spmd, %region_3.4_spmd} | conditional | flops 275613696 | bytes 9159250 | solution.py:75
  234.4 2.9 %fusion.7 = f32[256,2,8,128]{3,2,0,1:T(8,128)} fusion(f32[256,2,8,128]{3,2,0,1:T(8,128)} %get-tuple-element.403, s32[]{:T(128)S(6)} %select_n.30, f32[2,64,8,512]{3,2,1,0:T(8,128)S(1)} %get-tuple-element.533, f32[64,2,8]{2,0,1:T(8,128)S(1)} %get-tuple-element.531, pred[64,512]{1,0:T(8,128)(4,1)S(1)} %compare_and_fusion, ...), kind=kOutput, calls=%fused_computation.10 | convolution fusion | flops 137101312 | bytes 3604484 | tf_op jit(solution)/shard_map/while/body/eval_jaxpr/while/body/eval_jaxpr/cond/branch_1_fun/qkgn,nkd->qkgd/dot_general | solution.py:63
  239.9 5.2 %psum.7 = f32[256]{0:T(256)} all-reduce(f32[256]{0:T(256)S(1)} %bitcast.42), channel_id=1, replica_groups=mesh['groups'=2,'ctx'=8,'head'=2] {'head'}, use_global_device_ids=true, to_apply=%region_8.9 | all-reduce | flops 256 | bytes 2048 | tf_op jit(solution)/shard_map/psum | solution.py:92
  (196 shorter events, 77.4 us)
Async XLA Ops:
  7.2 232.3 %copy-start = (bf16[2,8,128]{2,1,0:T(8,128)(2,1)S(1)}, bf16[2,8,128]{2,1,0:T(8,128)(2,1)}, u32[]{:S(2)}) copy-start(bf16[2,8,128]{2,1,0:T(8,128)(2,1)} %param.15) | copy-start | bytes 12292
  7.2 4.7 %copy-start.2 = (s32[256]{0:T(256)S(1)}, s32[256]{0:T(256)}, u32[]{:S(2)}) copy-start(s32[256]{0:T(256)} %param.14) | copy-start | bytes 3076
  7.2 41.5 %all-gather.4.cloned.1.call-start = ((), (), s32[]{:S(2)}) async-start(), calls=%async_computation | async-start | bytes 1179648 | tf_op jit(solution)/shard_map/all_gather | solution.py:19
  8.8 81.0 %all-gather.6.cloned.1.call-start = ((), (), s32[]{:S(2)}) async-start(), calls=%async_computation.1 | async-start | bytes 1179648 | tf_op jit(solution)/shard_map/all_gather | solution.py:20
  239.5 5.6 %copy-start.1 = (bf16[256,2,8,128]{3,2,1,0:T(8,128)(2,1)}, bf16[256,2,8,128]{3,2,1,0:T(8,128)(2,1)S(1)}, u32[]{:S(2)}) copy-start(bf16[256,2,8,128]{3,2,1,0:T(8,128)(2,1)S(1)} %fusion.22) | copy-start | bytes 3145732
Sparse Core Ops, SparseCore 0:
  10.8 37.8 all-gather.3
  50.9 38.9 all-gather.5
where the time goes:
time: 254 us; the launch traced here: 252 us
  waiting for transfers between devices  65.1 us (26%)
  loops' own time  63.2 us (25%)
  local copies, waits for them, and re-layouts  43.9 us (17%)
  matrix products  35.4 us (14%)
  blocking collectives  18.1 us (7%)
  between operations  14.1 us (6%)
  other arithmetic  12.1 us (5%)
    another operation x4, loops' own time, key_step(): return lax.fori_loop(0, tile_count, query_step, state)  62.3 us
    all_gather x1, waiting for transfers between devices, attend(): value_piece = lax.all_gather(values, 'ctx', axis=0, tiled=True)  41.2 us
    dot_general x10, matrix products, compute(): jnp.einsum('qkgn,nkd->qkgd', weights.astype(jnp.bfloat16), value_block, p...  28.4 us
    all_gather x1, waiting for transfers between devices, attend(): key_piece = lax.all_gather(keys, 'ctx', axis=0, tiled=True)  23.9 us
    all_gather x1, blocking collectives, attend(): seg_piece = lax.all_gather(segments, 'ctx', axis=0, tiled=True)  12.9 us
    slice x16, local copies, waits for them, and re-layouts, query_step(): seg_block[0] <= tile_seg[-1]  10.4 us
    slice x16, local copies, waits for them, and re-layouts, query_step(): tile_pos[-1]  10.4 us
    slice x16, local copies, waits for them, and re-layouts, query_step(): key_pos[0] <= tile_pos[-1]  9.5 us
  transfers between devices with their start and end apart: 2, of which 2 were waited for; matrix products, arithmetic and copies ran while one was open for 1% of the time, Pallas kernels for 0%

commit v1 on v0

v1 whole, which is shorter than its diff:
```python
import functools
import math

import jax
import jax.numpy as jnp
from jax import lax
from jax.experimental import pallas as pl
from jax.experimental.pallas import tpu as pltpu
from jax.sharding import PartitionSpec as P

HIDDEN = -1e30
LABEL_ROWS = 16


def pack(keys, values, segments):
    rows = keys.shape[0]
    lanes = math.prod(keys.shape[1:])
    label_lines = -(-rows // lanes)
    labels = (segments + 1).astype(keys.dtype)
    labels = jnp.pad(labels, (0, label_lines * lanes - rows)).reshape(label_lines, lanes)
    labels = jnp.pad(labels, ((0, -label_lines % LABEL_ROWS), (0, 0)))
    return jnp.concatenate([keys.reshape(rows, lanes), values.reshape(rows, lanes), labels], axis=0)


def attend_kernel(sizes, scale, *refs):
    rows, heads, group, dim, tile_pos, count = sizes
    seg_ref, query_ref, weight_ref = refs[:3]
    block_refs = refs[3 : 3 + count]
    out_ref, score_ref, partial_ref = refs[3 + count :]
    per_pos = heads * group
    tile = tile_pos * per_pos
    lanes = heads * dim
    row_head = (lax.broadcasted_iota(jnp.int32, (tile, dim), 0) % per_pos) // group
    key_pos = lax.broadcasted_iota(jnp.int32, (1, rows), 1)
    first_seg = seg_ref[0]
    weight = weight_ref[...].astype(jnp.float32)

    def labels_of(ref):
        lines = -(-rows // lanes)
        grid = ref[2 * rows : 2 * rows + LABEL_ROWS * (-(-lines // LABEL_ROWS)), :].astype(jnp.float32)
        return jnp.concatenate([grid[n : n + 1, :] for n in range(lines)], axis=1)[:, :rows].astype(jnp.int32)

    def step(index, carry):
        start = pl.multiple_of(index * tile, tile)
        query = query_ref[pl.ds(start, tile), :]
        wide = jnp.concatenate(
            [jnp.where(row_head == h, query, jnp.zeros_like(query)) for h in range(heads)], axis=1
        )
        scores = []
        top = None
        for back, ref in enumerate(block_refs):
            labels = labels_of(ref)
            bias = []
            for p in range(tile_pos):
                pos = index * tile_pos + p
                seg = seg_ref[pos]
                if back == 0:
                    seen = (labels == seg + 1) & (key_pos <= pos)
                else:
                    wanted = jnp.where(seg == first_seg, seg + 1, -1)
                    seen = labels == wanted
                bias.append(jnp.broadcast_to(jnp.where(seen, 0.0, HIDDEN), (per_pos, rows)))
            part = lax.dot_general(
                wide, ref[:rows, :], (((1,), (1,)), ((), ())), preferred_element_type=jnp.float32
            )
            part = part + jnp.concatenate(bias, axis=0)
            scores.append(part)
            part_top = jnp.max(part, axis=1, keepdims=True)
            top = part_top if top is None else jnp.maximum(top, part_top)
        total = jnp.zeros((tile, 1), jnp.float32)
        acc = jnp.zeros((tile, lanes), jnp.float32)
        for part, ref in zip(scores, block_refs):
            weights = jnp.exp2((part - top) * scale)
            total = total + jnp.sum(weights, axis=1, keepdims=True)
            acc = acc + jnp.dot(
                weights.astype(jnp.bfloat16), ref[rows : 2 * rows, :], preferred_element_type=jnp.float32
            )
        mine = acc[:, :dim]
        for h in range(1, heads):
            mine = jnp.where(row_head == h, acc[:, h * dim : (h + 1) * dim], mine)
        attended = (mine / total).astype(jnp.bfloat16)
        out_ref[pl.ds(start, tile), :] = attended
        product = attended.astype(jnp.float32).reshape(tile_pos, per_pos, dim) * weight
        partial_ref[pl.ds(pl.multiple_of(index * tile_pos, tile_pos), tile_pos), :] = jnp.sum(product, axis=1)
        return carry

    lax.fori_loop(0, rows // tile_pos, step, 0)
    score_ref[...] = lax.dot_general(
        jnp.ones((8, dim), jnp.float32),
        partial_ref[...],
        (((1,), (1,)), ((), ())),
        preferred_element_type=jnp.float32,
        precision=lax.Precision.HIGHEST,
    )


def local(devices, queries, keys, values, segments, score_weight):
    rows, heads, group, dim = queries.shape
    reach = rows * devices // 2
    back = min(devices - 1, -(-(reach - 1) // rows))

    def shift(array, by):
        return lax.ppermute(array, "ctx", [(i, i + by) for i in range(devices - by)])

    blocks = [pack(keys, values, segments)]
    for distance in range(1, back + 1):
        blocks.append(shift(blocks[max(distance - 2, 0)], min(distance, 2)))

    per_pos = heads * group
    tile_pos = min(16, rows)
    vmem = pl.BlockSpec(memory_space=pltpu.VMEM)
    sizes = (rows, heads, group, dim, tile_pos, len(blocks))
    attended, score = pl.pallas_call(
        functools.partial(attend_kernel, sizes, math.log2(math.e) / math.sqrt(dim)),
        out_shape=(
            jax.ShapeDtypeStruct((rows * per_pos, dim), jnp.bfloat16),
            jax.ShapeDtypeStruct((8, rows), jnp.float32),
        ),
        in_specs=[pl.BlockSpec(memory_space=pltpu.SMEM)] + [vmem] * (2 + len(blocks)),
        out_specs=(vmem, vmem),
        scratch_shapes=[pltpu.VMEM((rows, dim), jnp.float32)],
        compiler_params=pltpu.CompilerParams(vmem_limit_bytes=48 * 1024 * 1024),
    )(segments, queries.reshape(rows * per_pos, dim), score_weight.reshape(per_pos, dim), *blocks)
    score = score[0]
    score = score + lax.ppermute(score, "head", [(0, 1), (1, 0)])
    return attended.reshape(queries.shape), score


def solution(mesh):
    return jax.shard_map(
        functools.partial(local, mesh.shape["ctx"]),
        mesh=mesh,
        in_specs=(
            P(("groups", "ctx"), "head", None, None),
            P(("groups", "ctx"), "head", None),
            P(("groups", "ctx"), "head", None),
            P(("groups", "ctx")),
            P("head", None, None),
        ),
        out_specs=(P(("groups", "ctx"), "head", None, None), P(("groups", "ctx"))),
        check_vma=False,
    )
```

time: 254 us -> 51.4 us (0.20)
  the two profiles are of different devices: /device:TPU:27 before, /device:TPU:29 now
where the time goes in v1:
time: 51.4 us; the launch traced here: 51.2 us
  waiting for transfers between devices  22.3 us (43%)
  Pallas kernels  18.5 us (36%)
  starting transfers between devices  6.7 us (13%)
  local copies, waits for them, and re-layouts  1.69 us (3%)
  other arithmetic  1.36 us (3%)
  between operations  0.69 us (1%)
    ppermute x4, waiting for transfers between devices, shift(): lax.ppermute(array, 'ctx', [(i, i + by) for i in range(devices - by)])  21.4 us
    pallas_call x1, Pallas kernels, local(): pl.pallas_call(functools.partial(attend_kernel, sizes, math.log2(math.e)...  18.5 us
    ppermute x4, starting transfers between devices, shift(): lax.ppermute(array, 'ctx', [(i, i + by) for i in range(devices - by)])  5.16 us
    ppermute x1, starting transfers between devices, local(): score = score + lax.ppermute(score, 'head', [(0, 1), (1, 0)])  1.55 us
  transfers between devices with their start and end apart: 5, of which 4 were waited for; matrix products, arithmetic and copies ran while one was open for 0% of the time, Pallas kernels for 0%

profile of v1, /device:TPU:29, one launch (start us, length us, event | category | flops | bytes accessed | tf_op | source)
XLA Modules:
  0.0 51.2 jit_solution(11445570166365597573)
XLA Ops:
  0.6 0.0 copy-start
  0.6 0.8 %add_convert_fusion = bf16[256]{0:T(256)(128)(2,1)S(1)} fusion(s32[256]{0:T(256)} %refs_0_.1), kind=kLoop, calls=%fused_computation.5 | loop fusion | flops 512 | bytes 1536 | tf_op jit(solution)/shard_map/convert_element_type | solution.py:19
  1.4 1.0 %copy_bitcast_fusion = (bf16[256,256]{1,0:T(8,128)(2,1)S(1)}, bf16[256,256]{1,0:T(8,128)(2,1)S(1)}) fusion(bf16[32,8,2,128]{3,2,1,0:T(2,128)(2,1)} %bitcast.12, bf16[32,8,2,128]{3,2,1,0:T(2,128)(2,1)} %bitcast.13), kind=kLoop, calls=%fused_computation.3 | loop fusion | bytes 524288 | tf_op jit(solution)/shard_map/reshape | solution.py:22
  2.4 0.0 copy-start.1
  2.5 1.3 %collective-permute-start.1 = (bf16[528,256]{1,0:T(8,128)(2,1)S(1)}, bf16[528,256]{1,0:T(8,128)(2,1)S(1)}, u32[]{:S(2)}, u32[]{:S(2)}) collective-permute-start(bf16[528,256]{1,0:T(8,128)(2,1)S(1)} %fusion.1.refs_3_), channel_id=1, source_target_pairs={{0,4},{2,6},{4,8},{6,10},{8,12},{10,14},{1,5},{3,7},{5,9},{7,11},{... | collective-permute-start | bytes 811016 | tf_op jit(solution)/shard_map/ppermute | solution.py:103
  3.8 1.3 %collective-permute-start = (bf16[528,256]{1,0:T(8,128)(2,1)S(1)}, bf16[528,256]{1,0:T(8,128)(2,1)S(1)}, u32[]{:S(2)}, u32[]{:S(2)}) collective-permute-start(bf16[528,256]{1,0:T(8,128)(2,1)S(1)} %fusion.1.refs_3_), channel_id=1, source_target_pairs={{0,2},{2,4},{4,6},{6,8},{8,10},{10,12},{12,14},{1,3},{3,5},{5,7},{... | collective-permute-start | bytes 811016 | tf_op jit(solution)/shard_map/ppermute | solution.py:103
  5.1 6.6 %collective-permute-done.1.refs_5_ = bf16[528,256]{1,0:T(8,128)(2,1)S(1)} collective-permute-done((bf16[528,256]{1,0:T(8,128)(2,1)S(1)}, bf16[528,256]{1,0:T(8,128)(2,1)S(1)}, u32[]{:S(2)}, u32[]{:S(2)}) %collective-permute-start.1) | collective-permute-done | bytes 270368 | tf_op jit(solution)/shard_map/ppermute | solution.py:103
  11.7 1.3 %collective-permute-start.3 = (bf16[528,256]{1,0:T(8,128)(2,1)S(1)}, bf16[528,256]{1,0:T(8,128)(2,1)S(1)}, u32[]{:S(2)}, u32[]{:S(2)}) collective-permute-start(bf16[528,256]{1,0:T(8,128)(2,1)S(1)} %collective-permute-done.1.refs_5_), channel_id=1, source_target_pairs={{0,4},{2,6},{4,8},{6,10},{8,12},{10,14},{1,5},{3,7},{5,9},{7,11},{... | collective-permute-start | bytes 811016 | tf_op jit(solution)/shard_map/ppermute | solution.py:103
  13.0 0.0 collective-permute-done.refs_4_
  13.0 1.3 %collective-permute-start.2 = (bf16[528,256]{1,0:T(8,128)(2,1)S(1)}, bf16[528,256]{1,0:T(8,128)(2,1)S(1)}, u32[]{:S(2)}, u32[]{:S(2)}) collective-permute-start(bf16[528,256]{1,0:T(8,128)(2,1)S(1)} %collective-permute-done.refs_4_), channel_id=1, source_target_pairs={{0,4},{2,6},{4,8},{6,10},{8,12},{10,14},{1,5},{3,7},{5,9},{7,11},{... | collective-permute-start | bytes 811016 | tf_op jit(solution)/shard_map/ppermute | solution.py:103
  14.3 9.0 %collective-permute-done.3.refs_7_ = bf16[528,256]{1,0:T(8,128)(2,1)S(1)} collective-permute-done((bf16[528,256]{1,0:T(8,128)(2,1)S(1)}, bf16[528,256]{1,0:T(8,128)(2,1)S(1)}, u32[]{:S(2)}, u32[]{:S(2)}) %collective-permute-start.3) | collective-permute-done | bytes 270368 | tf_op jit(solution)/shard_map/ppermute | solution.py:103
  23.3 5.8 %collective-permute-done.2.refs_6_ = bf16[528,256]{1,0:T(8,128)(2,1)S(1)} collective-permute-done((bf16[528,256]{1,0:T(8,128)(2,1)S(1)}, bf16[528,256]{1,0:T(8,128)(2,1)S(1)}, u32[]{:S(2)}, u32[]{:S(2)}) %collective-permute-start.2) | collective-permute-done | bytes 270368 | tf_op jit(solution)/shard_map/ppermute | solution.py:103
  29.1 0.0 copy-start.2
  29.1 0.0 copy-done
  29.1 0.0 copy-done.1
  29.1 0.7 %copy-done.2 = s32[256]{0:T(256)S(1)} copy-done((s32[256]{0:T(256)S(1)}, s32[256]{0:T(256)}, u32[]{:S(2)}) %copy-start.2) | copy-done | bytes 1048
  29.8 18.5 %shard_map.68 = (bf16[4096,128]{1,0:T(8,128)(2,1)}, f32[8,256]{1,0:T(8,128)S(1)}) custom-call(s32[256]{0:T(256)S(1)} %copy-done.2, bf16[4096,128]{1,0:T(8,128)(2,1)S(1)} %bitcast.10, bf16[16,128]{1,0:T(8,128)(2,1)S(1)} %bitcast.11, bf16[528,256]{1,0:T(8,128)(2,1)S(1)} %fusion.1.refs_3_, bf16[528,256]{1,0:T(8,128)(2,1)S(1)} %collective-permute-done.refs_4_, ...), custom_call_target="tpu_custom_call" | custom-call | tf_op jit(solution)/shard_map/pallas_call | solution.py:113
  48.2 1.5 %collective-permute-start.4 = (f32[256]{0:T(256)S(1)}, f32[256]{0:T(256)S(1)}, u32[]{:S(2)}, u32[]{:S(2)}) collective-permute-start(f32[256]{0:T(256)S(1)} %bitcast.14), channel_id=1, source_target_pairs={{0,1},{1,0},{2,3},{3,2},{4,5},{5,4},{6,7},{7,6},{8,9},{9,8},{10,11... | collective-permute-start | bytes 3080 | tf_op jit(solution)/shard_map/ppermute | solution.py:125
  49.8 0.8 %collective-permute-done.4 = f32[256]{0:T(256)S(1)} collective-permute-done((f32[256]{0:T(256)S(1)}, f32[256]{0:T(256)S(1)}, u32[]{:S(2)}, u32[]{:S(2)}) %collective-permute-start.4) | collective-permute-done | bytes 1056 | tf_op jit(solution)/shard_map/ppermute | solution.py:125
  50.6 0.6 %add.13 = f32[256]{0:T(256)} add(f32[256]{0:T(256)S(1)} %bitcast.15, f32[256]{0:T(256)S(1)} %collective-permute-done.4) | non-fusion elementwise | flops 256 | bytes 3072 | tf_op jit(solution)/shard_map/add | solution.py:125
  (3 shorter events, 0.0 us)
Async XLA Ops:
  0.6 28.5 %copy-start = (bf16[256,2,8,128]{3,2,1,0:T(8,128)(2,1)S(1)}, bf16[256,2,8,128]{3,2,1,0:T(8,128)(2,1)}, u32[]{:S(2)}) copy-start(bf16[256,2,8,128]{3,2,1,0:T(8,128)(2,1)} %param.5) | copy-start | bytes 3145732
  2.4 26.7 %copy-start.1 = (bf16[2,8,128]{2,1,0:T(8,128)(2,1)S(1)}, bf16[2,8,128]{2,1,0:T(8,128)(2,1)}, u32[]{:S(2)}) copy-start(bf16[2,8,128]{2,1,0:T(8,128)(2,1)} %param.9) | copy-start | bytes 12292
  2.5 9.2 %collective-permute-start.1 = (bf16[528,256]{1,0:T(8,128)(2,1)S(1)}, bf16[528,256]{1,0:T(8,128)(2,1)S(1)}, u32[]{:S(2)}, u32[]{:S(2)}) collective-permute-start(bf16[528,256]{1,0:T(8,128)(2,1)S(1)} %fusion.1.refs_3_), channel_id=1, source_target_pairs={{0,4},{2,6},{4,8},{6,10},{8,12},{10,14},{1,5},{3,7},{5,9},{7,11},{... | collective-permute-start | bytes 811016 | tf_op jit(solution)/shard_map/ppermute | solution.py:103
  3.8 9.2 %collective-permute-start = (bf16[528,256]{1,0:T(8,128)(2,1)S(1)}, bf16[528,256]{1,0:T(8,128)(2,1)S(1)}, u32[]{:S(2)}, u32[]{:S(2)}) collective-permute-start(bf16[528,256]{1,0:T(8,128)(2,1)S(1)} %fusion.1.refs_3_), channel_id=1, source_target_pairs={{0,2},{2,4},{4,6},{6,8},{8,10},{10,12},{12,14},{1,3},{3,5},{5,7},{... | collective-permute-start | bytes 811016 | tf_op jit(solution)/shard_map/ppermute | solution.py:103
  11.7 11.6 %collective-permute-start.3 = (bf16[528,256]{1,0:T(8,128)(2,1)S(1)}, bf16[528,256]{1,0:T(8,128)(2,1)S(1)}, u32[]{:S(2)}, u32[]{:S(2)}) collective-permute-start(bf16[528,256]{1,0:T(8,128)(2,1)S(1)} %collective-permute-done.1.refs_5_), channel_id=1, source_target_pairs={{0,4},{2,6},{4,8},{6,10},{8,12},{10,14},{1,5},{3,7},{5,9},{7,11},{... | collective-permute-start | bytes 811016 | tf_op jit(solution)/shard_map/ppermute | solution.py:103
  13.0 16.1 %collective-permute-start.2 = (bf16[528,256]{1,0:T(8,128)(2,1)S(1)}, bf16[528,256]{1,0:T(8,128)(2,1)S(1)}, u32[]{:S(2)}, u32[]{:S(2)}) collective-permute-start(bf16[528,256]{1,0:T(8,128)(2,1)S(1)} %collective-permute-done.refs_4_), channel_id=1, source_target_pairs={{0,4},{2,6},{4,8},{6,10},{8,12},{10,14},{1,5},{3,7},{5,9},{7,11},{... | collective-permute-start | bytes 811016 | tf_op jit(solution)/shard_map/ppermute | solution.py:103
  29.1 0.7 %copy-start.2 = (s32[256]{0:T(256)S(1)}, s32[256]{0:T(256)}, u32[]{:S(2)}) copy-start(s32[256]{0:T(256)} %refs_0_.1) | copy-start | bytes 3076
  48.2 2.4 %collective-permute-start.4 = (f32[256]{0:T(256)S(1)}, f32[256]{0:T(256)S(1)}, u32[]{:S(2)}, u32[]{:S(2)}) collective-permute-start(f32[256]{0:T(256)S(1)} %bitcast.14), channel_id=1, source_target_pairs={{0,1},{1,0},{2,3},{3,2},{4,5},{5,4},{6,7},{7,6},{8,9},{9,8},{10,11... | collective-permute-start | bytes 3080 | tf_op jit(solution)/shard_map/ppermute | solution.py:125

commit v2 on v1

v2 whole, which is shorter than its diff:
```python
import functools
import math

import jax
import jax.numpy as jnp
from jax import lax
from jax.experimental import pallas as pl
from jax.experimental.pallas import tpu as pltpu
from jax.sharding import PartitionSpec as P

HIDDEN = -1e30
LABEL_ROWS = 16


def pack(keys, values, segments):
    rows = keys.shape[0]
    lanes = math.prod(keys.shape[1:])
    label_lines = -(-rows // lanes)
    labels = (segments + 1).astype(keys.dtype)
    labels = jnp.pad(labels, (0, label_lines * lanes - rows)).reshape(label_lines, lanes)
    labels = jnp.pad(labels, ((0, -label_lines % LABEL_ROWS), (0, 0)))
    return jnp.concatenate([keys.reshape(rows, lanes), values.reshape(rows, lanes), labels], axis=0)


def attend_kernel(sizes, scale, first, last, *refs):
    rows, heads, group, dim, tile_pos, count = sizes
    refs = list(refs)
    seg_ref, query_ref = refs[:2]
    block_refs = refs[2 : 2 + count]
    refs = refs[2 + count :]
    if not first:
        old_top_ref, old_total_ref, old_acc_ref = refs[:3]
        refs = refs[3:]
    if last:
        weight_ref, out_ref, score_ref, partial_ref = refs
    else:
        top_ref, total_ref, acc_ref = refs
    per_pos = heads * group
    tile = tile_pos * per_pos
    half = tile_pos * group
    lanes = heads * dim
    key_pos = lax.broadcasted_iota(jnp.int32, (1, rows), 1)
    first_seg = seg_ref[0]

    def labels_of(ref):
        lines = -(-rows // lanes)
        grid = ref[2 * rows : 2 * rows + LABEL_ROWS * (-(-lines // LABEL_ROWS)), :].astype(jnp.float32)
        return jnp.concatenate([grid[n : n + 1, :] for n in range(lines)], axis=1)[:, :rows].astype(jnp.int32)

    def step(index, carry):
        start = pl.multiple_of(index * tile, tile)
        query = query_ref[pl.ds(start, tile), :].astype(jnp.float32).reshape(tile_pos, heads, group, dim)
        biases = []
        for n, ref in enumerate(block_refs):
            labels = labels_of(ref)
            bias = []
            for p in range(tile_pos):
                pos = index * tile_pos + p
                seg = seg_ref[pos]
                if first and n == 0:
                    seen = (labels == seg + 1) & (key_pos <= pos)
                else:
                    seen = labels == jnp.where(seg == first_seg, seg + 1, -1)
                bias.append(jnp.broadcast_to(jnp.where(seen, 0.0, HIDDEN), (group, rows)))
            biases.append(jnp.concatenate(bias, axis=0))
        if not first:
            old_top, old_total, old_acc = (
                ref[pl.ds(start, tile), :].reshape(tile_pos, heads, group, dim)
                for ref in (old_top_ref, old_total_ref, old_acc_ref)
            )
        tops, totals, accs = [], [], []
        for h in range(heads):
            at = slice(h * dim, (h + 1) * dim)
            query_h = query[:, h].reshape(half, dim).astype(jnp.bfloat16)
            top = None if first else old_top[:, h].reshape(half, dim)[:, :1]
            scores = []
            for ref, bias in zip(block_refs, biases):
                part = lax.dot_general(
                    query_h, ref[:rows, at], (((1,), (1,)), ((), ())), preferred_element_type=jnp.float32
                )
                part = part + bias
                scores.append(part)
                part_top = jnp.max(part, axis=1, keepdims=True)
                top = part_top if top is None else jnp.maximum(top, part_top)
            if first:
                total, acc = None, None
            else:
                factor = jnp.exp2((old_top[:, h].reshape(half, dim) - top) * scale)
                total = (old_total[:, h].reshape(half, dim) * factor)[:, :1]
                acc = old_acc[:, h].reshape(half, dim) * factor
            for part, ref in zip(scores, block_refs):
                weights = jnp.exp2((part - top) * scale)
                part_total = jnp.sum(weights, axis=1, keepdims=True)
                part_acc = jnp.dot(
                    weights.astype(jnp.bfloat16), ref[rows : 2 * rows, at], preferred_element_type=jnp.float32
                )
                total = part_total if total is None else total + part_total
                acc = part_acc if acc is None else acc + part_acc
            shape = (tile_pos, 1, group, dim)
            if last:
                accs.append((acc / total).reshape(shape))
            else:
                tops.append(jnp.broadcast_to(top, acc.shape).reshape(shape))
                totals.append(jnp.broadcast_to(total, acc.shape).reshape(shape))
                accs.append(acc.reshape(shape))

        def whole(parts):
            return jnp.concatenate(parts, axis=1).reshape(tile, dim)

        if last:
            attended = whole(accs).astype(jnp.bfloat16)
            out_ref[pl.ds(start, tile), :] = attended
            weight = weight_ref[...].astype(jnp.float32)
            product = attended.astype(jnp.float32).reshape(tile_pos, per_pos, dim) * weight
            partial_ref[pl.ds(pl.multiple_of(index * tile_pos, tile_pos), tile_pos), :] = jnp.sum(product, axis=1)
        else:
            top_ref[pl.ds(start, tile), :] = whole(tops)
            total_ref[pl.ds(start, tile), :] = whole(totals)
            acc_ref[pl.ds(start, tile), :] = whole(accs)
        return carry

    lax.fori_loop(0, rows // tile_pos, step, 0)
    if last:
        score_ref[...] = lax.dot_general(
            jnp.ones((8, dim), jnp.float32),
            partial_ref[...],
            (((1,), (1,)), ((), ())),
            preferred_element_type=jnp.float32,
            precision=lax.Precision.HIGHEST,
        )


def attend(shape, segments, query, blocks, state, weight):
    rows, heads, group, dim = shape
    per_pos = heads * group
    tile_pos = math.gcd(rows, 64)
    vmem = pl.BlockSpec(memory_space=pltpu.VMEM)
    first, last = state is None, weight is not None
    operands = [segments, query, *blocks, *(state or ()), *((weight,) if last else ())]
    flat = (rows * per_pos, dim)
    if last:
        out_shape = (jax.ShapeDtypeStruct(flat, jnp.bfloat16), jax.ShapeDtypeStruct((8, rows), jnp.float32))
    else:
        out_shape = (jax.ShapeDtypeStruct(flat, jnp.float32),) * 3
    work = 4 * rows * per_pos * dim * rows * len(blocks)
    return pl.pallas_call(
        functools.partial(
            attend_kernel,
            (rows, heads, group, dim, tile_pos, len(blocks)),
            math.log2(math.e) / math.sqrt(dim),
            first,
            last,
        ),
        out_shape=out_shape,
        in_specs=[pl.BlockSpec(memory_space=pltpu.SMEM)] + [vmem] * (len(operands) - 1),
        out_specs=(vmem,) * len(out_shape),
        scratch_shapes=[pltpu.VMEM((rows, dim), jnp.float32)] if last else [],
        cost_estimate=pl.CostEstimate(
            flops=work, bytes_accessed=rows * per_pos * dim * 8, transcendentals=work // (4 * dim)
        ),
        compiler_params=pltpu.CompilerParams(vmem_limit_bytes=32 * 1024 * 1024),
    )(*operands)


def local(devices, queries, keys, values, segments, score_weight):
    rows, heads, group, dim = queries.shape
    reach = rows * devices // 2
    back = min(devices - 1, -(-(reach - 1) // rows))

    def shift(array, by):
        return lax.ppermute(array, "ctx", [(i, i + by) for i in range(devices - by)])

    blocks = [pack(keys, values, segments)]
    for distance in range(1, back + 1):
        blocks.append(shift(blocks[max(distance - 2, 0)], min(distance, 2)))

    query = queries.reshape(rows * heads * group, dim)
    weight = score_weight.reshape(heads * group, dim)
    state = None
    for at in range(-1, back, 2):
        ends = at + 2 >= back
        state = attend(
            queries.shape, segments, query, blocks[max(at, 0) : at + 2], state, weight if ends else None
        )
    attended, score = state
    score = score[0]
    score = score + lax.ppermute(score, "head", [(0, 1), (1, 0)])
    return attended.reshape(queries.shape), score


def solution(mesh):
    return jax.shard_map(
        functools.partial(local, mesh.shape["ctx"]),
        mesh=mesh,
        in_specs=(
            P(("groups", "ctx"), "head", None, None),
            P(("groups", "ctx"), "head", None),
            P(("groups", "ctx"), "head", None),
            P(("groups", "ctx")),
            P("head", None, None),
        ),
        out_specs=(P(("groups", "ctx"), "head", None, None), P(("groups", "ctx"))),
        check_vma=False,
    )
```

time: 51.4 us -> 58.4 us (1.14)
  the two profiles are of different devices: /device:TPU:29 before, /device:TPU:5 now
where the time goes in v2:
time: 58.4 us; the launch traced here: 58.1 us
  Pallas kernels  31.3 us (54%)
  starting transfers between devices  16.7 us (29%)
  waiting for transfers between devices  5.31 us (9%)
  local copies, waits for them, and re-layouts  2.91 us (5%)
  other arithmetic  1.27 us (2%)
  between operations  0.72 us (1%)
    pallas_call x3, Pallas kernels, attend(): pl.pallas_call(functools.partial(attend_kernel, (rows, heads, group, dim,...  31.3 us
    ppermute x4, starting transfers between devices, shift(): lax.ppermute(array, 'ctx', [(i, i + by) for i in range(devices - by)])  13.7 us
    ppermute x4, waiting for transfers between devices, shift(): lax.ppermute(array, 'ctx', [(i, i + by) for i in range(devices - by)])  4.49 us
    ppermute x1, starting transfers between devices, local(): score = score + lax.ppermute(score, 'head', [(0, 1), (1, 0)])  2.97 us
    unnamed x6, local copies, waits for them, and re-layouts  1.9 us
  transfers between devices with their start and end apart: 5, of which 3 were waited for; matrix products, arithmetic and copies ran while one was open for 0% of the time, Pallas kernels for 30%

profile of v2, /device:TPU:5, one launch (start us, length us, event | category | flops | bytes accessed | tf_op | source)
XLA Modules:
  0.0 58.1 jit_solution(17813859733628964210)
XLA Ops:
  0.6 0.7 %add_convert_fusion = bf16[256]{0:T(256)(128)(2,1)S(1)} fusion(s32[256]{0:T(256)} %refs_0_.5), kind=kLoop, calls=%fused_computation.5 | loop fusion | flops 512 | bytes 1536 | tf_op jit(solution)/shard_map/convert_element_type | solution.py:19
  1.3 1.0 %copy_bitcast_fusion = (bf16[256,256]{1,0:T(8,128)(2,1)S(1)}, bf16[256,256]{1,0:T(8,128)(2,1)S(1)}) fusion(bf16[32,8,2,128]{3,2,1,0:T(2,128)(2,1)} %bitcast.14, bf16[32,8,2,128]{3,2,1,0:T(2,128)(2,1)} %bitcast.15), kind=kLoop, calls=%fused_computation.3 | loop fusion | bytes 524288 | tf_op jit(solution)/shard_map/reshape | solution.py:22
  2.4 3.1 %collective-permute-start = (bf16[528,256]{1,0:T(8,128)(2,1)S(1)}, bf16[528,256]{1,0:T(8,128)(2,1)S(1)}, u32[]{:S(2)}, u32[]{:S(2)}) collective-permute-start(bf16[528,256]{1,0:T(8,128)(2,1)S(1)} %fusion.1.refs_2_), channel_id=1, source_target_pairs={{0,2},{2,4},{4,6},{6,8},{8,10},{10,12},{12,14},{1,3},{3,5},{5,7},{... | collective-permute-start | bytes 811016 | tf_op jit(solution)/shard_map/ppermute | solution.py:171
  5.5 3.2 %collective-permute-start.2 = (bf16[528,256]{1,0:T(8,128)(2,1)S(1)}, bf16[528,256]{1,0:T(8,128)(2,1)S(1)}, u32[]{:S(2)}, u32[]{:S(2)}) collective-permute-start(bf16[528,256]{1,0:T(8,128)(2,1)S(1)} %fusion.1.refs_2_), channel_id=1, source_target_pairs={{0,4},{2,6},{4,8},{6,10},{8,12},{10,14},{1,5},{3,7},{5,9},{7,11},{... | collective-permute-start | bytes 811016 | tf_op jit(solution)/shard_map/ppermute | solution.py:171
  8.7 2.9 %collective-permute-done.refs_2_ = bf16[528,256]{1,0:T(8,128)(2,1)S(1)} collective-permute-done((bf16[528,256]{1,0:T(8,128)(2,1)S(1)}, bf16[528,256]{1,0:T(8,128)(2,1)S(1)}, u32[]{:S(2)}, u32[]{:S(2)}) %collective-permute-start) | collective-permute-done | bytes 270368 | tf_op jit(solution)/shard_map/ppermute | solution.py:171
  11.6 3.2 %collective-permute-start.1 = (bf16[528,256]{1,0:T(8,128)(2,1)S(1)}, bf16[528,256]{1,0:T(8,128)(2,1)S(1)}, u32[]{:S(2)}, u32[]{:S(2)}) collective-permute-start(bf16[528,256]{1,0:T(8,128)(2,1)S(1)} %collective-permute-done.refs_2_), channel_id=1, source_target_pairs={{0,4},{2,6},{4,8},{6,10},{8,12},{10,14},{1,5},{3,7},{5,9},{7,11},{... | collective-permute-start | bytes 811016 | tf_op jit(solution)/shard_map/ppermute | solution.py:171
  14.8 1.6 %collective-permute-done.2.refs_3_ = bf16[528,256]{1,0:T(8,128)(2,1)S(1)} collective-permute-done((bf16[528,256]{1,0:T(8,128)(2,1)S(1)}, bf16[528,256]{1,0:T(8,128)(2,1)S(1)}, u32[]{:S(2)}, u32[]{:S(2)}) %collective-permute-start.2) | collective-permute-done | bytes 270368 | tf_op jit(solution)/shard_map/ppermute | solution.py:171
  16.4 4.1 %collective-permute-start.3 = (bf16[528,256]{1,0:T(8,128)(2,1)S(1)}, bf16[528,256]{1,0:T(8,128)(2,1)S(1)}, u32[]{:S(2)}, u32[]{:S(2)}) collective-permute-start(bf16[528,256]{1,0:T(8,128)(2,1)S(1)} %collective-permute-done.2.refs_3_), channel_id=1, source_target_pairs={{0,4},{2,6},{4,8},{6,10},{8,12},{10,14},{1,5},{3,7},{5,9},{7,11},{... | collective-permute-start | bytes 811016 | tf_op jit(solution)/shard_map/ppermute | solution.py:171
  20.5 0.0 copy-start
  20.6 1.2 %copy-done = bf16[256,2,8,128]{3,2,1,0:T(8,128)(2,1)S(1)} copy-done((bf16[256,2,8,128]{3,2,1,0:T(8,128)(2,1)S(1)}, bf16[256,2,8,128]{3,2,1,0:T(8,128)(2,1)}, u32[]{:S(2)}) %copy-start) | copy-done | bytes 1048600
  21.8 0.0 copy-start.2
  21.8 0.7 %copy-done.2 = s32[256]{0:T(256)S(1)} copy-done((s32[256]{0:T(256)S(1)}, s32[256]{0:T(256)}, u32[]{:S(2)}) %copy-start.2) | copy-done | bytes 1048
  22.5 3.1 %shard_map.68 = (f32[4096,128]{1,0:T(8,128)S(1)}, f32[4096,128]{1,0:T(8,128)S(1)}, f32[4096,128]{1,0:T(8,128)S(1)}) custom-call(s32[256]{0:T(256)S(1)} %copy-done.2, bf16[4096,128]{1,0:T(8,128)(2,1)S(1)} %bitcast.10, bf16[528,256]{1,0:T(8,128)(2,1)S(1)} %fusion.1.refs_2_), custom_call_target="tpu_custom_call" | custom-call | flops 536870912 | bytes 4194304 | tf_op jit(solution)/shard_map/pallas_call | solution.py:146
  25.5 0.0 copy-start.1
  25.6 14.3 %shard_map.69 = (f32[4096,128]{1,0:T(8,128)S(1)}, f32[4096,128]{1,0:T(8,128)S(1)}, f32[4096,128]{1,0:T(8,128)S(1)}) custom-call(s32[256]{0:T(256)S(1)} %copy-done.2, bf16[4096,128]{1,0:T(8,128)(2,1)S(1)} %bitcast.11, bf16[528,256]{1,0:T(8,128)(2,1)S(1)} %collective-permute-done.refs_2_, bf16[528,256]{1,0:T(8,128)(2,1)S(1)} %collective-permute-done.2.refs_3_, ...), custom_call_target="tpu_custom_call" | custom-call | flops 1073741824 | bytes 4194304 | tf_op jit(solution)/shard_map/pallas_call | solution.py:146
  39.9 0.0 collective-permute-done.1.refs_2_
  39.9 0.0 collective-permute-done.3.refs_3_
  39.9 0.0 copy-done.1
  39.9 13.9 %shard_map.70 = (bf16[4096,128]{1,0:T(8,128)(2,1)}, f32[8,256]{1,0:T(8,128)S(1)}) custom-call(s32[256]{0:T(256)S(1)} %copy-done.2, bf16[4096,128]{1,0:T(8,128)(2,1)S(1)} %bitcast.12, bf16[528,256]{1,0:T(8,128)(2,1)S(1)} %collective-permute-done.1.refs_2_, bf16[528,256]{1,0:T(8,128)(2,1)S(1)} %collective-permute-done.3.refs_3_, ...), custom_call_target="tpu_custom_call" | custom-call | flops 1073741824 | bytes 4194304 | tf_op jit(solution)/shard_map/pallas_call | solution.py:146
  53.8 3.0 %collective-permute-start.4 = (f32[256]{0:T(256)S(1)}, f32[256]{0:T(256)S(1)}, u32[]{:S(2)}, u32[]{:S(2)}) collective-permute-start(f32[256]{0:T(256)S(1)} %bitcast.16), channel_id=1, source_target_pairs={{0,1},{1,0},{2,3},{3,2},{4,5},{5,4},{6,7},{7,6},{8,9},{9,8},{10,11... | collective-permute-start | bytes 3080 | tf_op jit(solution)/shard_map/ppermute | solution.py:187
  56.7 0.8 %collective-permute-done.4 = f32[256]{0:T(256)S(1)} collective-permute-done((f32[256]{0:T(256)S(1)}, f32[256]{0:T(256)S(1)}, u32[]{:S(2)}, u32[]{:S(2)}) %collective-permute-start.4) | collective-permute-done | bytes 1056 | tf_op jit(solution)/shard_map/ppermute | solution.py:187
  57.6 0.6 add.13
  (3 shorter events, 0.0 us)
Async XLA Ops:
  2.4 9.2 %collective-permute-start = (bf16[528,256]{1,0:T(8,128)(2,1)S(1)}, bf16[528,256]{1,0:T(8,128)(2,1)S(1)}, u32[]{:S(2)}, u32[]{:S(2)}) collective-permute-start(bf16[528,256]{1,0:T(8,128)(2,1)S(1)} %fusion.1.refs_2_), channel_id=1, source_target_pairs={{0,2},{2,4},{4,6},{6,8},{8,10},{10,12},{12,14},{1,3},{3,5},{5,7},{... | collective-permute-start | bytes 811016 | tf_op jit(solution)/shard_map/ppermute | solution.py:171
  5.5 10.9 %collective-permute-start.2 = (bf16[528,256]{1,0:T(8,128)(2,1)S(1)}, bf16[528,256]{1,0:T(8,128)(2,1)S(1)}, u32[]{:S(2)}, u32[]{:S(2)}) collective-permute-start(bf16[528,256]{1,0:T(8,128)(2,1)S(1)} %fusion.1.refs_2_), channel_id=1, source_target_pairs={{0,4},{2,6},{4,8},{6,10},{8,12},{10,14},{1,5},{3,7},{5,9},{7,11},{... | collective-permute-start | bytes 811016 | tf_op jit(solution)/shard_map/ppermute | solution.py:171
  11.6 28.3 %collective-permute-start.1 = (bf16[528,256]{1,0:T(8,128)(2,1)S(1)}, bf16[528,256]{1,0:T(8,128)(2,1)S(1)}, u32[]{:S(2)}, u32[]{:S(2)}) collective-permute-start(bf16[528,256]{1,0:T(8,128)(2,1)S(1)} %collective-permute-done.refs_2_), channel_id=1, source_target_pairs={{0,4},{2,6},{4,8},{6,10},{8,12},{10,14},{1,5},{3,7},{5,9},{7,11},{... | collective-permute-start | bytes 811016 | tf_op jit(solution)/shard_map/ppermute | solution.py:171
  16.4 23.4 %collective-permute-start.3 = (bf16[528,256]{1,0:T(8,128)(2,1)S(1)}, bf16[528,256]{1,0:T(8,128)(2,1)S(1)}, u32[]{:S(2)}, u32[]{:S(2)}) collective-permute-start(bf16[528,256]{1,0:T(8,128)(2,1)S(1)} %collective-permute-done.2.refs_3_), channel_id=1, source_target_pairs={{0,4},{2,6},{4,8},{6,10},{8,12},{10,14},{1,5},{3,7},{5,9},{7,11},{... | collective-permute-start | bytes 811016 | tf_op jit(solution)/shard_map/ppermute | solution.py:171
  20.5 1.2 %copy-start = (bf16[256,2,8,128]{3,2,1,0:T(8,128)(2,1)S(1)}, bf16[256,2,8,128]{3,2,1,0:T(8,128)(2,1)}, u32[]{:S(2)}) copy-start(bf16[256,2,8,128]{3,2,1,0:T(8,128)(2,1)} %param.5) | copy-start | bytes 3145732
  21.8 0.7 %copy-start.2 = (s32[256]{0:T(256)S(1)}, s32[256]{0:T(256)}, u32[]{:S(2)}) copy-start(s32[256]{0:T(256)} %refs_0_.5) | copy-start | bytes 3076
  25.5 14.3 %copy-start.1 = (bf16[2,8,128]{2,1,0:T(8,128)(2,1)S(1)}, bf16[2,8,128]{2,1,0:T(8,128)(2,1)}, u32[]{:S(2)}) copy-start(bf16[2,8,128]{2,1,0:T(8,128)(2,1)} %param.9) | copy-start | bytes 12292
  53.8 3.8 %collective-permute-start.4 = (f32[256]{0:T(256)S(1)}, f32[256]{0:T(256)S(1)}, u32[]{:S(2)}, u32[]{:S(2)}) collective-permute-start(f32[256]{0:T(256)S(1)} %bitcast.16), channel_id=1, source_target_pairs={{0,1},{1,0},{2,3},{3,2},{4,5},{5,4},{6,7},{7,6},{8,9},{9,8},{10,11... | collective-permute-start | bytes 3080 | tf_op jit(solution)/shard_map/ppermute | solution.py:187
